TPU v7x, 512 devices: a whole 4x4x16 slice. The times are simulated.
512 devices in a mesh: tower: 2 (over core), dp: 128 (over x, y_hi, z), mp: 2 (over y_lo).
Axes of the slice: x: 4, y: 4 (y_hi: 2, y_lo: 2; y = y_hi * 2 + y_lo), z: 16, core: 2. Of those that a mesh axis runs over, the one named last changes fastest.
Arguments:
- img_feats: bfloat16 [32768, 1536], P('dp'), may hold values from -6 to 6
- txt_feats: bfloat16 [32768, 1024], P('dp'), may hold values from -6 to 6
- w_img: bfloat16 [1536, 1152], P(None, 'mp'), may hold values from -0.15625 to 0.15625
- w_txt: bfloat16 [1024, 1152], P(None, 'mp'), may hold values from -0.1875 to 0.1875
- logit_scale: float32 [1], replicated, may hold values from 4 to 12
- logit_bias: float32 [1], replicated, may hold values from -4 to -1
Outputs:
- img_grad: float32 [1536, 1152], P(('tower', 'dp'), 'mp')
- txt_grad: float32 [1024, 1152], P(('tower', 'dp'), 'mp')
All inputs are finite; a program needn't handle non-finite values.
Results may differ from a plain program's by a relative error of at most 0.0035.
Values may be sent and summed in bfloat16 or wider, within the bound.
A program may use at most 64 MiB of HBM per device.

v0:
```python
import math

import jax
import jax.numpy as jnp
from jax import lax
from jax.sharding import PartitionSpec as P

HALF_WIN = 2


epsilon = 1e-06


def from_partner(block, axis, distance):
    count = lax.axis_size(axis)
    route = []
    for low in range(count):
        high = low | 1 << distance
        if high != low and high < count:
            route += [(low, high), (high, low)]
    return lax.ppermute(block, axis, route)


def shifted(value, axis, steps):
    count = lax.axis_size(axis)
    pairs = [(source, (source + steps) % count) for source in range(count)]
    return lax.ppermute(value, axis, pairs)


def arrange_rows(contrib, cycle_size, share_out):
    total_rows, width = contrib.shape
    share = total_rows // (2 * cycle_size)
    blocks = contrib.reshape(2, cycle_size, share, width).transpose(1, 0, 2, 3)
    blocks = jnp.pad(blocks, ((0, 0), (0, 0), (0, share_out - share), (0, 0)))
    return blocks.reshape(cycle_size * 2 * share_out, width)


def local(img_feats, txt_feats, w_img, w_txt, logit_scale, logit_bias):
    group_index = lax.axis_index("tower")
    member = lax.axis_index("mp")
    cycle_size = lax.axis_size("dp")
    tok_rows = img_feats.shape[0]
    half_rows = tok_rows // lax.axis_size("mp")
    projected = lax.cond(
        group_index == 0,
        lambda: jnp.dot(img_feats, w_img, preferred_element_type=jnp.float32),
        lambda: jnp.dot(txt_feats, w_txt, preferred_element_type=jnp.float32),
    )
    squares = lax.psum(jnp.sum(projected * projected, axis=1), "mp")
    radius = jnp.sqrt(squares + epsilon)
    normed = projected / radius[:, None]
    own_emb = lax.all_gather(normed.astype(jnp.bfloat16), "mp", axis=1, tiled=True)
    other_emb = from_partner(own_emb, "tower", 0)
    width = own_emb.shape[1]
    behind = []
    forward = []
    current = other_emb
    for step in range(HALF_WIN):
        current = shifted(current, "dp", 1)
        behind.append(current)
    current = other_emb
    for step in range(HALF_WIN):
        current = shifted(current, "dp", -1)
        forward.append(current)
    stacked = jnp.stack(behind[::-1] + [other_emb] + forward, axis=0)
    others = stacked.reshape(-1, width)
    own_rows = lax.dynamic_slice_in_dim(own_emb, member * half_rows, half_rows, 0)
    logits = (
        logit_scale[0]
        * lax.dot_general(
            own_rows, others, (((1,), (1,)), ((), ())), preferred_element_type=jnp.float32
        )
        + logit_bias[0]
    )
    columns = jnp.arange(others.shape[0])[None, :]
    row_ids = jnp.arange(half_rows)[:, None] + member * half_rows + HALF_WIN * tok_rows
    labels = jnp.where(columns == row_ids, jnp.float32(1.0), jnp.float32(-1.0))
    inv_scale = jnp.float32(1.0 / math.sqrt(tok_rows * cycle_size))
    coef = (-labels * jax.nn.sigmoid(-labels * logits) * inv_scale).astype(jnp.bfloat16)
    grad_rows = logit_scale[0] * jnp.dot(coef, others, preferred_element_type=jnp.float32)
    grad_unit = lax.all_to_all(grad_rows, "mp", split_axis=1, concat_axis=0, tiled=True)
    inner_dot = lax.psum(jnp.sum(normed * grad_unit, axis=1), "mp")
    grad_proj = ((grad_unit - normed * inner_dot[:, None]) / radius[:, None]).astype(jnp.bfloat16)
    img_share = w_img.shape[0] // (2 * cycle_size)
    txt_share = w_txt.shape[0] // (2 * cycle_size)
    cols_local = w_img.shape[1]

    def image_part():
        contrib = lax.dot_general(
            img_feats, grad_proj, (((0,), (0,)), ((), ())), preferred_element_type=jnp.float32
        )
        return arrange_rows(contrib, cycle_size, img_share)

    def text_part():
        contrib = lax.dot_general(
            txt_feats, grad_proj, (((0,), (0,)), ((), ())), preferred_element_type=jnp.float32
        )
        return arrange_rows(contrib, cycle_size, img_share)

    laid_out = lax.cond(group_index == 0, image_part, text_part)
    summed = lax.psum_scatter(laid_out, "dp", scatter_dimension=0, tiled=True)
    is_image = group_index == 0
    blank_img = jnp.zeros((img_share, cols_local), jnp.float32)
    blank_txt = jnp.zeros((txt_share, cols_local), jnp.float32)
    img_keep = jnp.where(is_image, summed[:img_share], blank_img)
    img_send = jnp.where(is_image, summed[img_share:], blank_img)
    txt_keep = jnp.where(is_image, blank_txt, summed[img_share : img_share + txt_share])
    txt_send = jnp.where(is_image, blank_txt, summed[:txt_share])
    received = from_partner((img_send, txt_send), "tower", 0)
    return (img_keep + received[0], txt_keep + received[1])


def solution(mesh):
    placed = (P("dp", None), P("dp", None), P(None, "mp"), P(None, "mp"), P(), P())
    return jax.shard_map(
        local,
        mesh=mesh,
        in_specs=placed,
        out_specs=(P(("tower", "dp"), "mp"), P(("tower", "dp"), "mp")),
        check_vma=False,
    )
```

profile of v0, /device:TPU:1, one launch (start us, length us, event | category | flops | bytes accessed | tf_op | source)
XLA Modules:
  0.0 1510.7 jit_solution(17470303295778718521)
XLA Ops:
  7.2 0.0 all-reduce.4.cloned.1.call-start
  7.2 2.0 conditional.2
  7.2 1.9 fusion.30
  9.2 0.1 multiply_reduce_fusion
  9.3 4.4 psum.14
  13.7 0.1 fusion.29
  13.8 6.3 all_gather.3
  20.1 0.3 copy.51
  20.3 10.9 collective-permute-start
  31.2 1.6 collective-permute-done
  32.8 1.9 collective-permute-start.1
  34.7 11.0 collective-permute-start.3
  45.8 11.5 collective-permute-done.1
  57.2 1.9 collective-permute-start.2
  60.4 0.0 collective-permute-done.3
  60.5 9.1 collective-permute-start.4
  69.5 9.2 collective-permute-done.2
  78.8 0.1 bitcast_dynamic-update-slice_fusion.3
  78.9 0.1 bitcast_dynamic-update-slice_fusion.2
  79.0 0.1 bitcast_dynamic-update-slice_fusion.1
  79.1 1.9 collective-permute-done.4
  81.0 0.1 bitcast_dynamic-update-slice_fusion
  81.1 1.6 copy-done.2
  82.7 5.3 convolution_multiply_fusion
  88.0 1.4 copy.52
  89.4 9.0 all_to_all.19
  98.4 0.1 fusion.11
  98.5 3.8 psum.15
  102.3 0.1 fusion.13
  102.4 0.0 copy-done
  102.5 0.0 copy-done.1
  102.5 13.7 conditional.3
  102.5 2.1 fusion.32
  104.6 2.8 reshape.26
  107.4 0.5 copy.62
  107.8 2.7 pad.3.clone
  110.6 5.6 reshape.27
  116.2 0.0 all-reduce.4.cloned.1.call-update
  116.2 1.3 dynamic-slice
  118.1 1291.7 %all-reduce.4.cloned.1.call-done = f32[1536,576]{1,0:T(8,128)} async-done(((f32[1536,576]{1,0:T(8,128)}), f32[1536,576]{1,0:T(8,128)}) %all-reduce.4.cloned.1.call-update) | async-done | bytes 3538960
  1409.9 0.7 dynamic-slice_select_fusion.2
  1410.6 87.7 %collective-permute-start.6 = (f32[4,576]{1,0:T(4,128)S(1)}, f32[4,576]{1,0:T(4,128)S(1)}, u32[]{:S(2)}, u32[]{:S(2)}) collective-permute-start(f32[4,576]{1,0:T(4,128)S(1)} %dynamic-slice_select_fusion.2), channel_id=1, source_target_pairs={{0,256},{256,0},{1,257},{257,1},{2,258},{258,2},{3,259},{259,3},{4... | collective-permute-start | bytes 27656 | tf_op jit(solution)/shard_map/ppermute | solution.py:21
  1498.4 0.8 dynamic-slice_select_fusion
  1499.2 1.9 collective-permute-start.5
  1501.1 0.0 collective-permute-done.6
  1501.1 1.4 fusion.23
  1502.5 0.0 collective-permute-done.5
  1502.5 1.4 fusion.22
  (6 shorter events, 0.1 us)
Async XLA Ops:
  7.2 1402.7 %all-reduce.4.cloned.1.call-start = ((), (), s32[]{:S(2)}) async-start(), calls=%async_computation.1 | async-start | bytes 7864320
  20.3 12.5 collective-permute-start
  32.8 24.4 %collective-permute-start.1 = (bf16[256,1152]{1,0:T(8,128)(2,1)S(1)}, bf16[256,1152]{1,0:T(8,128)(2,1)S(1)}, u32[]{:S(2)}, u32[]{:S(2)}) collective-permute-start(bf16[256,1152]{1,0:T(8,128)(2,1)S(1)} %collective-permute-done), channel_id=1, source_target_pairs={{0,2},{2,4},{4,6},{6,8},{8,10},{10,12},{12,14},{14,16},{16,18},{18... | collective-permute-start | bytes 1769480 | tf_op jit(solution)/shard_map/ppermute | solution.py:27
  34.7 25.7 %collective-permute-start.3 = (bf16[256,1152]{1,0:T(8,128)(2,1)S(1)}, bf16[256,1152]{1,0:T(8,128)(2,1)S(1)}, u32[]{:S(2)}, u32[]{:S(2)}) collective-permute-start(bf16[256,1152]{1,0:T(8,128)(2,1)S(1)} %collective-permute-done), channel_id=1, source_target_pairs={{0,254},{2,0},{4,2},{6,4},{8,6},{10,8},{12,10},{14,12},{16,14},{18... | collective-permute-start | bytes 1769480 | tf_op jit(solution)/shard_map/ppermute | solution.py:27
  57.2 21.6 %collective-permute-start.2 = (bf16[256,1152]{1,0:T(8,128)(2,1)S(1)}, bf16[256,1152]{1,0:T(8,128)(2,1)S(1)}, u32[]{:S(2)}, u32[]{:S(2)}) collective-permute-start(bf16[256,1152]{1,0:T(8,128)(2,1)S(1)} %collective-permute-done.1), channel_id=1, source_target_pairs={{0,2},{2,4},{4,6},{6,8},{8,10},{10,12},{12,14},{14,16},{16,18},{18... | collective-permute-start | bytes 1769480 | tf_op jit(solution)/shard_map/ppermute | solution.py:27
  60.5 20.5 %collective-permute-start.4 = (bf16[256,1152]{1,0:T(8,128)(2,1)S(1)}, bf16[256,1152]{1,0:T(8,128)(2,1)S(1)}, u32[]{:S(2)}, u32[]{:S(2)}) collective-permute-start(bf16[256,1152]{1,0:T(8,128)(2,1)S(1)} %collective-permute-done.3), channel_id=1, source_target_pairs={{0,254},{2,0},{4,2},{6,4},{8,6},{10,8},{12,10},{14,12},{16,14},{18... | collective-permute-start | bytes 1769480 | tf_op jit(solution)/shard_map/ppermute | solution.py:27
  81.1 1.6 copy-start.2
  88.0 14.5 copy-start
  88.0 14.5 copy-start.1
  1410.6 90.5 %collective-permute-start.6 = (f32[4,576]{1,0:T(4,128)S(1)}, f32[4,576]{1,0:T(4,128)S(1)}, u32[]{:S(2)}, u32[]{:S(2)}) collective-permute-start(f32[4,576]{1,0:T(4,128)S(1)} %dynamic-slice_select_fusion.2), channel_id=1, source_target_pairs={{0,256},{256,0},{1,257},{257,1},{2,258},{258,2},{3,259},{259,3},{4... | collective-permute-start | bytes 27656 | tf_op jit(solution)/shard_map/ppermute | solution.py:21
  1499.2 3.3 collective-permute-start.5
Sparse Core Ops, SparseCore 0:
  116.3 1293.5 all-reduce.3
where the time goes:
time: 1510 us
  waiting for transfers between devices  1320 us (87%)
  starting transfers between devices  124 us (8%)
  blocking collectives  23.5 us (2%)
  local copies, waits for them, and re-layouts  16.4 us (1%)
  between operations  16.2 us (1%)
    unnamed x2, waiting for transfers between devices  1290 us
    ppermute x3, starting transfers between devices, from_partner(): return lax.ppermute(block, axis, route)  101 us
  transfers between devices with their start and end apart: 8, of which 5 were waited for; matrix products, arithmetic and copies ran while one was open for 0% of the time, Pallas kernels for 0%

commit v1 on v0

v1 whole, which is shorter than its diff:
```python
import functools
import math

import jax
import jax.numpy as jnp
import numpy as np
from jax import lax
from jax.experimental import pallas as pl
from jax.experimental.pallas import tpu as pltpu
from jax.sharding import PartitionSpec as P

MESH = pl.DeviceIdType.MESH
HALF_WIN = 2
EPS = 1e-06
NX, NYH, CLS = 4, 2, 4
MSGS = 96
F32 = jnp.float32
BF16 = jnp.bfloat16


def row_order(width, dp, piece, padded):
    zh = dp // (NX * NYH * CLS)
    z_count = zh * CLS
    per_x = NYH * z_count * piece
    rows = 2 * CLS * zh * NYH * 2 * padded
    mat = np.zeros((rows, 4 * per_x), np.float32)
    for xr in range(2):
        for zl in range(CLS):
            for zg in range(zh):
                for yh in range(NYH):
                    for half in range(2):
                        for i in range(piece):
                            out = ((((xr * CLS + zl) * zh + zg) * NYH + yh) * 2 + half) * padded + i
                            col = half * 2 * per_x + xr * per_x + yh * z_count * piece + (zg * CLS + zl) * piece + i
                            mat[out, col] = 1.0
    return mat


def col_to_rows(col):
    n = col.shape[0]
    return jnp.transpose(jnp.broadcast_to(col, (n, 128)))[:8]


def rows_to_col(rows):
    n = rows.shape[1]
    return jnp.transpose(jnp.broadcast_to(rows[:1], (128, n)))[:, :1]


def dot_nt(a, b):
    return lax.dot_general(a, b, (((1,), (1,)), ((), ())), preferred_element_type=F32)


def dot_nn(a, b):
    return jnp.dot(a, b, preferred_element_type=F32)


def body(cfg, scale_ref, bias_ref, img_ref, txt_ref, wi_ref, wt_ref, pi_ref, pt_ref, out_img, out_txt, *scratch):
    (feats, weights, perm, feats_t, fx, normed, own, win, acc, sq_out, sq_in, inner_out, inner_in, ssem, rsem, lsem) = scratch[:16]
    rest = scratch[16:]
    dp, tok, d_img, d_txt, cols, chunks = cfg["dp"], cfg["tok"], cfg["d_img"], cfg["d_txt"], cfg["cols"], cfg["chunks"]
    zh_count = dp // (NX * NYH * CLS)
    z_count = zh_count * CLS
    half = tok // 2
    r_img, r_txt, pad = d_img // (2 * dp), d_txt // (2 * dp), cfg["pad"]
    xrows = CLS * zh_count * NYH * 2 * pad
    crow = xrows // CLS
    lrow = crow // zh_count
    names = ("ps", "pr", "gx", "cf", "cb", "l1", "s1", "l2", "st", "l3")
    buf = [dict(zip(names, rest[len(names) * q : len(names) * (q + 1)])) for q in range(len(chunks))]

    t, d, m = lax.axis_index("tower"), lax.axis_index("dp"), lax.axis_index("mp")
    x = d // (NYH * z_count)
    yh = (d // z_count) % NYH
    z = d % z_count
    zl, zg = z % CLS, z // CLS
    h = (m + yh) % 2

    def at(xx, yy, zz):
        return (xx * NYH + yy) * z_count + zz

    partner = (t, d, 1 - m)
    band_dev = {}
    for k in range(-HALF_WIN, HALF_WIN + 1):
        dk = (d + k + dp) % dp
        band_dev[k] = (1 - t, dk, (h + (dk // z_count) % NYH) % 2)
    x_dev = {j: (t, at((x + j) % NX, yh, z), m) for j in (1, 2, 3)}
    z_dev = {j: (t, at(x, yh, (z + j + z_count) % z_count), m) for j in (1, -1, 2, -2)}
    zg_dev = {j: (t, at(x, yh, ((zg + j) % zh_count) * CLS + zl), m) for j in range(1, zh_count)}
    fin_dev = {(1, 0): (1 - t, d, m), (0, 1): (t, at(x, 1 - yh, z), m), (1, 1): (1 - t, at(x, 1 - yh, z), m)}

    peers = [partner] + list(band_dev.values()) + list(x_dev.values()) + list(z_dev.values()) + list(zg_dev.values())
    peers += [fin_dev[0, 1], fin_dev[1, 1]]
    barrier = pltpu.get_barrier_semaphore()
    for dev in peers:
        pl.semaphore_signal(barrier, inc=1, device_id=dev, device_id_type=MESH)

    ids = {}
    started = []

    def copy(key, src, dst, dev):
        n = ids.setdefault(key, len(ids))
        return pltpu.make_async_remote_copy(
            src_ref=src, dst_ref=dst, send_sem=ssem.at[n], recv_sem=rsem.at[n], device_id=dev, device_id_type=MESH
        )

    def send(key, src, dst, dev):
        c = copy(key, src, dst, dev)
        c.start()
        started.append(c)

    def arrive(key, dst, dev):
        copy(key, dst, dst, dev).wait_recv()

    def loads(which):
        f, w, p, wide = ((img_ref, wi_ref, pi_ref, d_img), (txt_ref, wt_ref, pt_ref, d_txt))[which]
        pk = p.shape[1]
        return [
            pltpu.make_async_copy(f, feats.at[:, pl.ds(0, wide)], lsem.at[0]),
            pltpu.make_async_copy(w, weights.at[:, pl.ds(0, wide)], lsem.at[1]),
            pltpu.make_async_copy(p, perm.at[:, pl.ds(0, pk)], lsem.at[2]),
        ]

    def project(which):
        wide = (d_img, d_txt)[which]
        ls = loads(which)
        for c in ls:
            c.start()
        ls[0].wait()
        ls[1].wait()
        normed[...] = dot_nt(feats[:, :wide], weights[:, :wide])
        ls[2].wait()

    def reorder(which):
        wide = (d_img, d_txt)[which]
        pk = (pi_ref, pt_ref)[which].shape[1]
        for xp in range(2):
            a = xp * pk // 2
            b = wide // 2 + a
            part = dot_nt(perm[:, : pk // 2], feats[:, a : a + pk // 2])
            part = part + dot_nt(perm[:, pk // 2 : pk], feats[:, b : b + pk // 2])
            feats_t[xp * 2 * xrows : (xp + 1) * 2 * xrows, :] = part.astype(BF16)

    for which in range(2):
        pl.when(t == which)(functools.partial(project, which))

    proj = normed[...]
    squares = jnp.sum(proj * proj, axis=1, keepdims=True)
    sq_out[...] = col_to_rows(squares)
    pl.semaphore_wait(barrier, len(peers))
    send("sq", sq_out, sq_in, partner)

    for which in range(2):
        pl.when(t == which)(functools.partial(reorder, which))

    arrive("sq", sq_in, partner)
    inv_radius = 1.0 / jnp.sqrt(squares + rows_to_col(sq_in[...]) + EPS)
    unit = normed[...] * inv_radius
    normed[...] = unit
    own[m] = unit.astype(BF16)

    keep = pl.ds(pl.multiple_of(h * half, half), half)
    give = pl.ds(pl.multiple_of((1 - h) * half, half), half)
    order = (0, 1, -1, 2, -2)
    send("e0", own.at[m, give], own.at[m, give], partner)
    for k in order:
        send(("b", k, 0), own.at[m, keep], win.at[HALF_WIN - k, m], band_dev[k])
    send("e1", own.at[m, keep], own.at[m, keep], partner)
    for j in (1, 3, 2):
        xs = pl.ds(pl.multiple_of(((x + j) % NX) * xrows, xrows), xrows)
        send(("f", j), feats_t.at[xs], fx.at[x], x_dev[j])
    arrive("e0", own.at[1 - m, keep], partner)
    for k in order:
        send(("b", k, 1), own.at[1 - m, keep], win.at[HALF_WIN - k, 1 - m], band_dev[k])
    arrive("e1", own.at[1 - m, give], partner)

    scale, bias = scale_ref[0], bias_ref[0]
    inv_scale = F32(1.0 / math.sqrt(tok * dp))
    inner = jnp.zeros((tok, 1), F32)
    for n, k in enumerate(order):
        slot = HALF_WIN + k
        for part in range(2):
            arrive(("b", -k, part), win.at[slot, part], band_dev[k])
        dots = dot_nt(own[0], win[slot, 0]) + dot_nt(own[1], win[slot, 1])
        logits = scale * dots + bias
        if k == 0:
            rows = lax.broadcasted_iota(jnp.int32, (tok, half), 0)
            columns = lax.broadcasted_iota(jnp.int32, (tok, half), 1) + h * half
            labels = jnp.where(rows == columns, F32(1.0), F32(-1.0))
            coef = -labels * jax.nn.sigmoid(-labels * logits) * inv_scale
        else:
            coef = jax.nn.sigmoid(logits) * inv_scale
        coef = coef.astype(BF16)
        inner = inner + jnp.sum(coef.astype(F32) * dots, axis=1, keepdims=True)
        for c in range(2):
            term = dot_nn(coef, win[slot, c])
            if n:
                acc[c] += term
            else:
                acc[c] = term
    inner = inner * scale
    inner_out[...] = col_to_rows(inner)

    send("inner", inner_out, inner_in, partner)
    for q, (c0, w) in enumerate(chunks):
        b = buf[q]
        b["ps"][...] = (scale * acc[1 - m, :, c0 : c0 + w]).astype(BF16)
        send(("p", q), b["ps"], b["pr"], partner)
    arrive("inner", inner_in, partner)
    total_inner = inner + rows_to_col(inner_in[...])

    low, high = pl.ds(0, half), pl.ds(half, half)
    clow, chigh = pl.ds(0, crow // 2), pl.ds(crow // 2, crow // 2)
    left, right, across = (x + 3) % NX, (x + 1) % NX, (x + 2) % NX

    def stage_g(q):
        c0, w = chunks[q]
        b = buf[q]
        arrive(("p", q), b["pr"], partner)
        grad = scale * acc[m, :, c0 : c0 + w] + b["pr"][...].astype(F32)
        grad = (grad - normed[:, c0 : c0 + w] * total_inner) * inv_radius
        b["gx"][x] = grad.astype(BF16)
        send(("x", q, 1), b["gx"].at[x], b["gx"].at[x], x_dev[1])
        send(("x", q, 3), b["gx"].at[x], b["gx"].at[x], x_dev[3])

    def stage_x(q):
        gx = buf[q]["gx"]
        arrive(("x", q, 1), gx.at[left], x_dev[3])
        send(("y", q, 1), gx.at[left, low], gx.at[left, low], x_dev[1])
        arrive(("x", q, 3), gx.at[right], x_dev[1])
        send(("y", q, 3), gx.at[right, high], gx.at[right, high], x_dev[3])

    def stage_c(q):
        b = buf[q]
        gx, cf, cb = b["gx"], b["cf"], b["cb"]
        mine = pl.ds(pl.multiple_of(x * xrows, xrows), xrows)
        total = dot_nn(feats_t[mine], gx[x])
        if q == 0:
            for j in (1, 3, 2):
                arrive(("f", j), fx.at[(x + 4 - j) % NX], x_dev[4 - j])
        total += dot_nn(fx[left], gx[left])
        total += dot_nn(fx[right], gx[right])
        arrive(("y", q, 1), gx.at[across, low], x_dev[3])
        arrive(("y", q, 3), gx.at[across, high], x_dev[1])
        total += dot_nn(fx[across], gx[across])
        for c in range(CLS):
            piece = total[c * crow : (c + 1) * crow]
            cf[c] = piece
            cb[c] = piece.astype(BF16)
        send(("l1", q, 2), cb.at[(zl + 2) % CLS, clow], b["l1"].at[2, clow], z_dev[2])
        send(("l1", q, -2), cb.at[(zl + 2) % CLS, chigh], b["l1"].at[2, chigh], z_dev[-2])
        send(("l1", q, 1), cb.at[(zl + 1) % CLS], b["l1"].at[0], z_dev[1])
        send(("l1", q, -1), cb.at[(zl + 3) % CLS], b["l1"].at[1], z_dev[-1])

    def stage_1(q):
        b = buf[q]
        arrive(("l1", q, 1), b["l1"].at[0], z_dev[-1])
        arrive(("l1", q, -1), b["l1"].at[1], z_dev[1])
        arrive(("l1", q, 2), b["l1"].at[2, clow], z_dev[-2])
        arrive(("l1", q, -2), b["l1"].at[2, chigh], z_dev[2])
        total = b["cf"][zl] + b["l1"][0].astype(F32) + b["l1"][1].astype(F32) + b["l1"][2].astype(F32)
        for g in range(zh_count):
            b["s1"][g] = total[g * lrow : (g + 1) * lrow]
        for j in range(1, zh_count):
            send(("l2", q, j), b["s1"].at[(zg + j) % zh_count], b["l2"].at[j], zg_dev[j])

    def stage_2(q):
        b = buf[q]
        total = b["s1"][zg]
        for j in range(1, zh_count):
            arrive(("l2", q, j), b["l2"].at[j], zg_dev[zh_count - j])
            total = total + b["l2"][j]
        for p in range(2 * NYH):
            b["st"][p // 2, p % 2, :pad] = total[p * pad : (p + 1) * pad]
        for (dt, dy), dev in fin_dev.items():
            tt, yy = (t + dt) % 2, (yh + dy) % 2
            send(("l3", q, dt, dy), b["st"].at[yy, tt], b["l3"].at[t, dy], dev)
        b["l3"][t, 0] = b["st"][yh, t]

    def stage_3(q):
        c0, w = chunks[q]
        b = buf[q]
        for (dt, dy), dev in fin_dev.items():
            arrive(("l3", q, dt, dy), b["l3"].at[(t + dt) % 2, dy], dev)
        out_img[:, c0 : c0 + w] = (b["l3"][0, 0] + b["l3"][0, 1])[:r_img]
        out_txt[:, c0 : c0 + w] = (b["l3"][1, 0] + b["l3"][1, 1])[:r_txt]

    stages = (stage_g, stage_x, stage_c, stage_1, stage_2, stage_3)
    for step in range(len(stages) + len(chunks) - 1):
        for q in range(len(chunks)):
            if 0 <= step - q < len(stages):
                stages[step - q](q)
    for c in started:
        c.wait_send()


def local(cfg, img_feats, txt_feats, w_img, w_txt, logit_scale, logit_bias):
    dp = lax.axis_size("dp")
    tok, d_img = img_feats.shape
    d_txt = txt_feats.shape[1]
    cols = w_img.shape[1]
    r_img, r_txt = d_img // (2 * dp), d_txt // (2 * dp)
    pad = max(r_img, r_txt)
    chunks = cfg["chunks"](cols)
    cfg = dict(dp=dp, tok=tok, d_img=d_img, d_txt=d_txt, cols=cols, chunks=chunks, pad=pad)
    perm_img = jnp.asarray(row_order(d_img, dp, r_img, pad), BF16)
    perm_txt = jnp.asarray(row_order(d_txt, dp, r_txt, pad), BF16)
    zh_count = dp // (NX * NYH * CLS)
    half = tok // 2
    xrows = CLS * zh_count * NYH * 2 * pad
    crow = xrows // CLS
    lrow = crow // zh_count
    wide = max(d_img, d_txt)
    scratch = [
        pltpu.VMEM((tok, wide), BF16),
        pltpu.VMEM((cols, wide), BF16),
        pltpu.VMEM((2 * xrows, max(perm_img.shape[1], perm_txt.shape[1])), BF16),
        pltpu.VMEM((NX * xrows, tok), BF16),
        pltpu.VMEM((NX, xrows, tok), BF16),
        pltpu.VMEM((tok, cols), F32),
        pltpu.VMEM((2, tok, cols), BF16),
        pltpu.VMEM((2 * HALF_WIN + 1, 2, half, cols), BF16),
        pltpu.VMEM((2, tok, cols), F32),
        pltpu.VMEM((8, tok), F32),
        pltpu.VMEM((8, tok), F32),
        pltpu.VMEM((8, tok), F32),
        pltpu.VMEM((8, tok), F32),
        pltpu.SemaphoreType.DMA((MSGS,)),
        pltpu.SemaphoreType.DMA((MSGS,)),
        pltpu.SemaphoreType.DMA((3,)),
    ]
    for _, w in chunks:
        scratch += [
            pltpu.VMEM((tok, w), BF16),
            pltpu.VMEM((tok, w), BF16),
            pltpu.VMEM((NX, tok, w), BF16),
            pltpu.VMEM((CLS, crow, w), F32),
            pltpu.VMEM((CLS, crow, w), BF16),
            pltpu.VMEM((3, crow, w), BF16),
            pltpu.VMEM((zh_count, lrow, w), F32),
            pltpu.VMEM((zh_count, lrow, w), F32),
            pltpu.VMEM((NYH, 2, 8, w), F32),
            pltpu.VMEM((2, NYH, 8, w), F32),
        ]
    anyspace = pl.BlockSpec(memory_space=pl.ANY)
    smem = pl.BlockSpec(memory_space=pltpu.SMEM)
    vmem = pl.BlockSpec(memory_space=pltpu.VMEM)
    return pl.pallas_call(
        functools.partial(body, cfg),
        out_shape=(jax.ShapeDtypeStruct((r_img, cols), F32), jax.ShapeDtypeStruct((r_txt, cols), F32)),
        in_specs=[smem, smem] + [anyspace] * 6,
        out_specs=(vmem, vmem),
        scratch_shapes=scratch,
        compiler_params=pltpu.CompilerParams(
            collective_id=0, has_side_effects=True, vmem_limit_bytes=44 * 1024 * 1024
        ),
    )(logit_scale, logit_bias, img_feats, txt_feats, w_img.T, w_txt.T, perm_img, perm_txt)


def column_chunks(cols):
    if cols <= 256:
        return ((0, cols),)
    return ((0, 256), (256, cols - 256))


def solution(mesh):
    placed = (P("dp", None), P("dp", None), P(None, "mp"), P(None, "mp"), P(), P())
    return jax.shard_map(
        functools.partial(local, dict(chunks=column_chunks)),
        mesh=mesh,
        in_specs=placed,
        out_specs=(P(("tower", "dp"), "mp"), P(("tower", "dp"), "mp")),
        check_vma=False,
    )
```

time: 1510 us -> 96.6 us (0.06)
  the two profiles are of different devices: /device:TPU:1 before, /device:TPU:9 now
where the time goes in v1:
time: 96.6 us; the launch traced here: 96.2 us
  Pallas kernels  85.8 us (89%)
  local copies, waits for them, and re-layouts  8.52 us (9%)
  between operations  1.94 us (2%)
    pallas_call x1, Pallas kernels, local(): pl.pallas_call(functools.partial(body, cfg), out_shape=(jax.ShapeDtypeStr...  85.8 us
    unnamed x14, local copies, waits for them, and re-layouts  8.52 us

profile of v1, /device:TPU:9, one launch (start us, length us, event | category | flops | bytes accessed | tf_op | source)
XLA Modules:
  0.0 96.2 jit_solution(12765148789236893570)
XLA Ops:
  1.9 0.0 copy-start
  1.9 1.5 %copy-done = bf16[1536,576]{0,1:T(8,128)(2,1)S(1)} copy-done((bf16[1536,576]{0,1:T(8,128)(2,1)S(1)}, bf16[1536,576]{0,1:T(8,128)(2,1)}, u32[]{:S(2)}) %copy-start) | copy-done | bytes 1769496
  3.4 0.0 copy-start.1
  3.4 1.3 %copy-done.1 = bf16[1024,576]{0,1:T(8,128)(2,1)S(1)} copy-done((bf16[1024,576]{0,1:T(8,128)(2,1)S(1)}, bf16[1024,576]{0,1:T(8,128)(2,1)}, u32[]{:S(2)}) %copy-start.1) | copy-done | bytes 1179672
  4.7 0.0 copy-start.2
  4.7 1.3 %copy-done.2 = bf16[768,768]{1,0:T(8,128)(2,1)S(1)} copy-done((bf16[768,768]{1,0:T(8,128)(2,1)S(1)}, bf16[768,768]{1,0:T(8,128)(2,1)}, u32[]{:S(2)}) %copy-start.2) | copy-done | bytes 1179672
  5.9 0.0 copy-start.3
  5.9 1.1 %copy-done.3 = bf16[256,1536]{1,0:T(8,128)(2,1)S(1)} copy-done((bf16[256,1536]{1,0:T(8,128)(2,1)S(1)}, bf16[256,1536]{1,0:T(8,128)(2,1)}, u32[]{:S(2)}) %copy-start.3) | copy-done | bytes 786456
  7.1 0.0 copy-start.4
  7.1 1.1 %copy-done.4 = bf16[768,512]{1,0:T(8,128)(2,1)S(1)} copy-done((bf16[768,512]{1,0:T(8,128)(2,1)S(1)}, bf16[768,512]{1,0:T(8,128)(2,1)}, u32[]{:S(2)}) %copy-start.4) | copy-done | bytes 786456
  8.2 0.0 copy-start.5
  8.2 1.0 %copy-done.5 = bf16[256,1024]{1,0:T(8,128)(2,1)S(1)} copy-done((bf16[256,1024]{1,0:T(8,128)(2,1)S(1)}, bf16[256,1024]{1,0:T(8,128)(2,1)}, u32[]{:S(2)}) %copy-start.5) | copy-done | bytes 524312
  9.3 85.8 %shard_map.95 = (f32[6,576]{1,0:T(8,128)S(1)}, f32[4,576]{1,0:T(4,128)S(1)}) custom-call(f32[1]{0:T(128)S(6)} %copy.12.scale_ref, f32[1]{0:T(128)S(6)} %copy.13.bias_ref, bf16[256,1536]{1,0:T(8,128)(2,1)S(1)} %copy-done.3, bf16[256,1024]{1,0:T(8,128)(2,1)S(1)} %copy-done.5, bf16[576,1536]{1,0:T(8,128)(2,1)S(1)} %bitcast.2, bf16[576,1024]{1,0:T(8,128)(2,1)S(1)} %bitcast.3, ...), custom_call_target="tpu_custom_call" | custom-call | tf_op jit(solution)/shard_map/pallas_call | solution.py:347
  95.0 0.6 copy.14
  95.6 0.6 copy.15
Async XLA Ops:
  1.9 1.5 %copy-start = (bf16[1536,576]{0,1:T(8,128)(2,1)S(1)}, bf16[1536,576]{0,1:T(8,128)(2,1)}, u32[]{:S(2)}) copy-start(bf16[1536,576]{0,1:T(8,128)(2,1)} %param.10) | copy-start | bytes 5308420
  3.4 1.3 %copy-start.1 = (bf16[1024,576]{0,1:T(8,128)(2,1)S(1)}, bf16[1024,576]{0,1:T(8,128)(2,1)}, u32[]{:S(2)}) copy-start(bf16[1024,576]{0,1:T(8,128)(2,1)} %param.11) | copy-start | bytes 3538948
  4.7 1.3 %copy-start.2 = (bf16[768,768]{1,0:T(8,128)(2,1)S(1)}, bf16[768,768]{1,0:T(8,128)(2,1)}, u32[]{:S(2)}) copy-start(bf16[768,768]{1,0:T(8,128)(2,1)} %constant.4.clone.pi_ref) | copy-start | bytes 3538948
  5.9 1.1 %copy-start.3 = (bf16[256,1536]{1,0:T(8,128)(2,1)S(1)}, bf16[256,1536]{1,0:T(8,128)(2,1)}, u32[]{:S(2)}) copy-start(bf16[256,1536]{1,0:T(8,128)(2,1)} %img_ref.1) | copy-start | bytes 2359300
  7.1 1.1 %copy-start.4 = (bf16[768,512]{1,0:T(8,128)(2,1)S(1)}, bf16[768,512]{1,0:T(8,128)(2,1)}, u32[]{:S(2)}) copy-start(bf16[768,512]{1,0:T(8,128)(2,1)} %constant.5.clone.pt_ref) | copy-start | bytes 2359300
  8.2 1.0 %copy-start.5 = (bf16[256,1024]{1,0:T(8,128)(2,1)S(1)}, bf16[256,1024]{1,0:T(8,128)(2,1)}, u32[]{:S(2)}) copy-start(bf16[256,1024]{1,0:T(8,128)(2,1)} %txt_ref.1) | copy-start | bytes 1572868

commit v2 on v0

v2 whole, which is shorter than its diff:
```python
import functools
import math

import jax
import jax.numpy as jnp
from jax import lax
from jax.experimental import pallas as pl
from jax.experimental.pallas import tpu as pltpu
from jax.sharding import PartitionSpec as P

MESH = pl.DeviceIdType.MESH
EPS = 1e-06
NX, NYH, CLS = 4, 2, 4
MSGS = 128
F32 = jnp.float32
BF16 = jnp.bfloat16


def dot_nt(a, b):
    return lax.dot_general(a, b, (((1,), (1,)), ((), ())), preferred_element_type=F32)


def dot_nn(a, b):
    return jnp.dot(a, b, preferred_element_type=F32)


def col_to_rows(col):
    n = col.shape[0]
    return jnp.transpose(jnp.broadcast_to(col, (n, 128)))[:8]


def body(cfg, scale_ref, bias_ref, img_ref, txt_ref, wi_ref, wt_ref, out_img, out_txt, *scratch):
    (smem, feats, weights, perm, feats_t, fx, normed, own_t, own_n, win, acc) = scratch[:11]
    (sq_out, sq_in, inner_out, inner_in, ssem, rsem, lsem) = scratch[11:18]
    rest = scratch[18:]
    dp, tok, widths, chunks = cfg["dp"], cfg["tok"], cfg["widths"], cfg["chunks"]
    zgs = dp // (NX * NYH * CLS)
    zs = zgs * CLS
    half = tok // 2
    pieces = [w // (2 * dp) for w in widths]
    names = ("ps", "pr", "gx", "cb", "l1", "xf", "xs", "xr", "st", "l2")
    buf = [dict(zip(names, rest[len(names) * q : len(names) * (q + 1)])) for q in range(len(chunks))]

    t, d, m = lax.axis_index("tower"), lax.axis_index("dp"), lax.axis_index("mp")
    x = d // (NYH * zs)
    yh = (d // zs) % NYH
    z = d % zs
    zl, zg = z % CLS, z // CLS
    h = (m + yh) % 2

    def at(xx, yy, zz):
        return (xx * NYH + yy) * zs + zz

    def along_z(dz, dy):
        return (t, at(x, (yh + dy) % NYH, (z + dz + zs) % zs), m)

    def block(k):
        b = (d + k + dp) % dp
        return b, (h + (b // zs) % NYH) % 2

    partner = (t, d, 1 - m)
    cross = {k: (1 - t,) + block(k) for k in (0, 1, -1)}
    onward = {k: (t,) + block(k) for k in (1, -1)}
    x_dev = {j: (t, at((x + j) % NX, yh, z), m) for j in (1, 2, 3)}
    two = {}
    for dy in range(NYH):
        yy = (yh + dy) % NYH
        two[dy] = (t, at(x, yy, (z + 2 - 4 * yy + zs) % zs), m)
    last = {(j, dt): ((t + dt) % 2, at(x, yh, ((zg + j) % zgs) * CLS + zl), m) for j in range(zgs) for dt in range(2)}
    del last[0, 0]

    peers = [cross[0], cross[1], cross[-1], onward[1], onward[-1]]
    peers += [along_z(dz, dy) for dz in (1, -1, 2, -2) for dy in range(NYH)]
    peers += [dev for (j, dt), dev in last.items() if j]
    peers += list(x_dev.values()) + [along_z(0, 1), partner]
    barrier = pltpu.get_barrier_semaphore()
    for dev in peers:
        pl.semaphore_signal(barrier, inc=1, device_id=dev, device_id_type=MESH)

    ids = {}
    started = {0: [], 1: [], None: []}

    def copy(key, src, dst, dev):
        n = ids.setdefault(key, len(ids))
        return pltpu.make_async_remote_copy(
            src_ref=src, dst_ref=dst, send_sem=ssem.at[n], recv_sem=rsem.at[n], device_id=dev, device_id_type=MESH
        )

    def send(key, src, dst, dev, which=None, like=None):
        copy(key, src, dst, dev).start()
        started[which].append((key, like or (lambda: dst)))

    def arrive(key, dst):
        copy(key, dst, dst, partner).wait_recv()

    def by_tower(fn, *args):
        for which in range(2):
            pl.when(t == which)(functools.partial(fn, which, *args))

    def project(which):
        f, w, wide = (img_ref, txt_ref)[which], (wi_ref, wt_ref)[which], widths[which]
        loads = [
            pltpu.make_async_copy(f, feats.at[:, pl.ds(0, wide)], lsem.at[0]),
            pltpu.make_async_copy(w, weights.at[:, pl.ds(0, wide)], lsem.at[1]),
            pltpu.make_async_copy(scale_ref, smem.at[0], lsem.at[2]),
            pltpu.make_async_copy(bias_ref, smem.at[1], lsem.at[3]),
        ]
        for c in loads:
            c.start()
        for c in loads:
            c.wait()
        normed[...] = dot_nt(weights[:, :wide], feats[:, :wide])

    def reorder(which):
        wide, r = widths[which], pieces[which]
        n = wide // 2
        row = lax.broadcasted_iota(jnp.int32, (n, 128), 0)
        p = (row * ((65536 + r - 1) // r)) >> 16
        i = row - p * r
        zbits = zgs.bit_length() - 1
        hf, g, y, c, xr = p & 1, (p >> 1) & (zgs - 1), (p >> (1 + zbits)) & 1, (p >> (2 + zbits)) & 3, p >> (4 + zbits)
        col = ((hf * 2 + xr) * NYH + y) * (zs * r) + (g * CLS + c) * r + i
        lane = lax.broadcasted_iota(jnp.int32, (n, 128), 1)
        for c0 in range(0, n, 128):
            cw = min(128, n - c0)
            perm[:n, c0 : c0 + cw] = jnp.where(col == lane + c0, F32(1.0), F32(0.0)).astype(BF16)[:, :cw]
        for xp in range(2):
            a = xp * n // 2
            part = dot_nt(perm[:n, : n // 2], feats[:, a : a + n // 2])
            part = part + dot_nt(perm[:n, n // 2 : n], feats[:, n + a : n + a + n // 2])
            feats_t[xp * n : (xp + 1) * n, :] = part.astype(BF16)
        rows = wide // NX
        for j in (1, 3, 2):
            xs = pl.ds(pl.multiple_of(((x + j) % NX) * rows, 16), rows)
            send(("f", j), feats_t.at[xs], fx.at[x, pl.ds(0, rows)], x_dev[j], which, lambda: fx.at[0, pl.ds(0, rows)])

    by_tower(project)
    squares = jnp.sum(normed[...] * normed[...], axis=0, keepdims=True)
    sq_out[...] = jnp.broadcast_to(squares, sq_out.shape)
    pl.semaphore_wait(barrier, len(peers))
    send("sq", sq_out, sq_in, partner)
    arrive("sq", sq_in)
    inv_radius = 1.0 / jnp.sqrt(squares + sq_in[:1] + EPS)
    unit = normed[...] * inv_radius
    normed[...] = unit
    unit = unit.astype(BF16)
    for th in range(2):
        own_t[m, th] = unit[:, th * half : (th + 1) * half]

    send("e0", own_t.at[m, 1 - h], own_t.at[m, 1 - h], partner)
    for s in (1, -1, 0):
        send(("b", s, 0), own_t.at[m, h], win.at[2 - s, m], cross[s])
    send("e1", own_t.at[m, h], own_t.at[m, h], partner)
    by_tower(reorder)
    arrive("e0", own_t.at[1 - m, h])
    for s in (1, -1, 0):
        send(("b", s, 1), own_t.at[1 - m, h], win.at[2 - s, 1 - m], cross[s])
    for f in range(2):
        for s in (1, -1):
            side = cross[-s][2]
            c = side if f == 0 else 1 - side
            arrive(("b", s, f), win.at[2 - s, c])
            send(("w", s, f), win.at[2 - s, c], win.at[2 - 2 * s, c], onward[s])
        if f == 0:
            arrive("e1", own_t.at[1 - m, 1 - h])
            for c in range(2):
                for th in range(2):
                    own_n[c, th * half : (th + 1) * half, :] = jnp.transpose(own_t[c, th])

    scale, bias = smem[0, 0], smem[1, 0]
    inv_scale = F32(1.0 / math.sqrt(tok * dp))
    inner = jnp.zeros((tok, half), F32)
    for n, k in enumerate((0, 1, -1, 2, -2)):
        slot = 2 + k
        if k == 0:
            for f in range(2):
                arrive(("b", 0, f), win.at[slot, f])
        if abs(k) == 2:
            for f in range(2):
                arrive(("w", -k // 2, f), win.at[slot, f])
        dots = dot_nn(own_n[0], win[slot, 0]) + dot_nn(own_n[1], win[slot, 1])
        logits = scale * dots + bias
        if k == 0:
            rows = lax.broadcasted_iota(jnp.int32, (tok, half), 0)
            columns = lax.broadcasted_iota(jnp.int32, (tok, half), 1) + h * half
            labels = jnp.where(rows == columns, F32(1.0), F32(-1.0))
            coef = -labels * jax.nn.sigmoid(-labels * logits) * inv_scale
        else:
            coef = jax.nn.sigmoid(logits) * inv_scale
        coef = coef.astype(BF16)
        inner = inner + coef.astype(F32) * dots
        for c in range(2):
            term = dot_nt(win[slot, c], coef)
            if n:
                acc[c] += term
            else:
                acc[c] = term
    inner_out[...] = scale * col_to_rows(jnp.sum(inner, axis=1, keepdims=True))
    send("inner", inner_out, inner_in, partner)
    for q, (c0, w, _) in enumerate(chunks):
        b = buf[q]
        b["ps"][...] = (scale * acc[1 - m, c0 : c0 + w]).astype(BF16)
        send(("p", q), b["ps"], b["pr"], partner)
    arrive("inner", inner_in)
    total_inner = inner_out[:1] + inner_in[:1]

    def stage_g(q):
        c0, w, z_first = chunks[q]
        b = buf[q]
        arrive(("p", q), b["pr"])
        grad = scale * acc[m, c0 : c0 + w] + b["pr"][...].astype(F32)
        grad = (grad - normed[c0 : c0 + w] * total_inner) * inv_radius
        own = 0 if z_first else x
        b["gx"][own] = grad.astype(BF16)
        if z_first:
            by_tower(part_products, q)
        else:
            for j in (2, 1, 3):
                send(("x", q, j), b["gx"].at[x], b["gx"].at[x], x_dev[j])

    def send_classes(which, q, br):
        cb, l1 = buf[q]["cb"], buf[q]["l1"]
        rows = pl.ds(0, br)

        def go(slot, c, dy, dev):
            send(("l1", q, slot), cb.at[c % CLS, (yh + dy) % NYH, :, rows], l1.at[slot, :, rows], dev, which, lambda: l1.at[0, :, pl.ds(0, br)])

        for dy in (1, 0):
            go(4 + dy, zl + 2, dy, two[dy])
        for dy in (1, 0):
            go(0 + dy, zl + 1, dy, along_z(1, dy))
            go(2 + dy, zl + 3, dy, along_z(-1, dy))
        go(6, zl, 1, along_z(0, 1))

    def part_products(which, q):
        b = buf[q]
        rows = widths[which] // NX
        br = rows // (CLS * NYH)
        for xx in range(NX):
            total = dot_nt(feats_t[xx * rows : (xx + 1) * rows], b["gx"][0]).astype(BF16)
            for c in range(CLS):
                for y in range(NYH):
                    o = (c * NYH + y) * br
                    b["cb"][c, y, xx, :br] = total[o : o + br]
        send_classes(which, q, br)

    def x_products(which, q):
        b = buf[q]
        gx = b["gx"]
        rows = widths[which] // NX
        br = rows // (CLS * NYH)
        mine = pl.ds(pl.multiple_of(x * rows, 16), rows)
        total = dot_nt(feats_t[mine], gx[x])
        for j in (1, 3, 2):
            src = (x + NX - j) % NX
            if q == first_x:
                arrive(("f", j), fx.at[src, pl.ds(0, rows)])
            arrive(("x", q, j), gx.at[src])
            total += dot_nt(fx[src, :rows], gx[src])
        total = total.astype(BF16)
        for c in range(CLS):
            for y in range(NYH):
                o = (c * NYH + y) * br
                b["cb"][c, y, 0, :br] = total[o : o + br]
        send_classes(which, q, br)

    def class_sum(which, q):
        b = buf[q]
        z_first = chunks[q][2]
        r = pieces[which]
        br = widths[which] // (NX * CLS * NYH)
        for slot in range(7):
            arrive(("l1", q, slot), b["l1"].at[slot, :, pl.ds(0, br)])

        def total(xx):
            s = b["cb"][zl, yh, xx, :br].astype(F32)
            for slot in range(7):
                s = s + b["l1"][slot, xx, :br].astype(F32)
            return s

        if z_first:
            for xx in range(NX):
                s = total(xx)
                b["xf"][xx, :br] = s
                b["xs"][xx, :br] = s.astype(BF16)
            for j in (2, 1, 3):
                src = b["xs"].at[(x + j) % NX, pl.ds(0, br)]
                like = lambda: b["xr"].at[0, pl.ds(0, br)]
                send(("xr", q, j), src, b["xr"].at[j, pl.ds(0, br)], x_dev[j], which, like)
        else:
            send_last(which, q, total(0))

    def x_sum(which, q):
        b = buf[q]
        br = widths[which] // (NX * CLS * NYH)
        s = b["xf"][x, :br]
        for j in (1, 3, 2):
            arrive(("xr", q, j), b["xr"].at[j, pl.ds(0, br)])
            s = s + b["xr"][j, :br].astype(F32)
        send_last(which, q, s)

    def send_last(which, q, s):
        st, l2 = buf[q]["st"], buf[q]["l2"]
        r = pieces[which]
        for g in range(zgs):
            for hf in range(2):
                o = (g * 2 + hf) * r
                st[g, hf, :r] = s[o : o + r]
        l2[t, 0] = st[zg, t]
        for (j, dt), dev in last.items():
            send(("l2", q, j, dt), st.at[(zg + j) % zgs, (t + dt) % 2], l2.at[t, j], dev, which, lambda: l2.at[0, 0])

    def finish(q):
        c0, w, _ = chunks[q]
        l2 = buf[q]["l2"]
        for j, dt in last:
            arrive(("l2", q, j, dt), l2.at[(t + dt) % 2, j])
        a, b = l2[0, 0], l2[1, 0]
        for j in range(1, zgs):
            a, b = a + l2[0, j], b + l2[1, j]
        out_img[:, c0 : c0 + w] = a[: pieces[0]]
        out_txt[:, c0 : c0 + w] = b[: pieces[1]]

    first_x = min(q for q, c in enumerate(chunks) if not c[2])
    for stage, q in cfg["order"](chunks):
        if stage == "g":
            stage_g(q)
        elif stage == "c":
            by_tower(x_products, q)
        elif stage == "1":
            by_tower(class_sum, q)
        elif stage == "x":
            by_tower(x_sum, q)
        else:
            finish(q)

    def drain(which):
        for key, like in started[which]:
            copy(key, like(), like(), partner).wait_send()

    by_tower(drain)
    drain(None)


def local(cfg, img_feats, txt_feats, w_img, w_txt, logit_scale, logit_bias):
    dp = lax.axis_size("dp")
    tok = img_feats.shape[0]
    widths = (img_feats.shape[1], txt_feats.shape[1])
    cols = w_img.shape[1]
    chunks = cfg["chunks"](cols)
    cfg = dict(cfg, dp=dp, tok=tok, widths=widths, chunks=chunks)
    zgs = dp // (NX * NYH * CLS)
    half = tok // 2
    wide = max(widths)
    rows = wide // NX
    br = rows // (CLS * NYH)
    pieces = [w // (2 * dp) for w in widths]
    scratch = [
        pltpu.SMEM((2, 1), F32),
        pltpu.VMEM((tok, wide), BF16),
        pltpu.VMEM((cols, wide), BF16),
        pltpu.VMEM((wide // 2, wide // 2), BF16),
        pltpu.VMEM((wide, tok), BF16),
        pltpu.VMEM((NX, rows, tok), BF16),
        pltpu.VMEM((cols, tok), F32),
        pltpu.VMEM((2, 2, cols, half), BF16),
        pltpu.VMEM((2, tok, cols), BF16),
        pltpu.VMEM((5, 2, cols, half), BF16),
        pltpu.VMEM((2, cols, tok), F32),
        pltpu.VMEM((8, tok), F32),
        pltpu.VMEM((8, tok), F32),
        pltpu.VMEM((8, tok), F32),
        pltpu.VMEM((8, tok), F32),
        pltpu.SemaphoreType.DMA((MSGS,)),
        pltpu.SemaphoreType.DMA((MSGS,)),
        pltpu.SemaphoreType.DMA((4,)),
    ]
    for _, w, z_first in chunks:
        xb = NX if z_first else 1
        xz = br if z_first else 16
        scratch += [
            pltpu.VMEM((w, tok), BF16),
            pltpu.VMEM((w, tok), BF16),
            pltpu.VMEM((1 if z_first else NX, w, tok), BF16),
            pltpu.VMEM((CLS, NYH, xb, br, w), BF16),
            pltpu.VMEM((7, xb, br, w), BF16),
            pltpu.VMEM((NX, xz, w), F32),
            pltpu.VMEM((NX, xz, w), BF16),
            pltpu.VMEM((NX, xz, w), BF16),
            pltpu.VMEM((zgs, 2, 8, w), F32),
            pltpu.VMEM((2, zgs, 8, w), F32),
        ]
    hbm = pl.BlockSpec(memory_space=pltpu.HBM)
    vmem = pl.BlockSpec(memory_space=pltpu.VMEM)
    return pl.pallas_call(
        functools.partial(body, cfg),
        out_shape=tuple(jax.ShapeDtypeStruct((r, cols), F32) for r in pieces),
        in_specs=[hbm] * 6,
        out_specs=(vmem, vmem),
        scratch_shapes=scratch,
        compiler_params=pltpu.CompilerParams(
            collective_id=0, has_side_effects=True, vmem_limit_bytes=61 * 1024 * 1024
        ),
    )(logit_scale, logit_bias, img_feats, txt_feats, w_img.T, w_txt.T)


def column_chunks(cols):
    return ((0, 256, False), (256, cols - 256, False))


def stage_order(chunks):
    steps = ["gc1l", "g1xl"]
    out = []
    for step in range(4 + len(chunks)):
        for q, c in enumerate(chunks):
            if 0 <= step - q < 4:
                out.append((steps[c[2]][step - q], q))
    return out


def solution(mesh):
    placed = (P("dp", None), P("dp", None), P(None, "mp"), P(None, "mp"), P(), P())
    return jax.shard_map(
        functools.partial(local, dict(chunks=column_chunks, order=stage_order)),
        mesh=mesh,
        in_specs=placed,
        out_specs=(P(("tower", "dp"), "mp"), P(("tower", "dp"), "mp")),
        check_vma=False,
    )
```

time: 1510 us -> 80.9 us (0.05)
  waiting for transfers between devices: 1320 us -> 0 us
  starting transfers between devices: 124 us -> 0 us
  Pallas kernels: 0 us -> 75.4 us
  blocking collectives: 23.5 us -> 0 us
    unnamed x2 -> x0, waiting for transfers between devices: 1290 us -> none
    ppermute x7 -> x0, starting transfers between devices: 124 us -> none  [the longest x3 101 us: from_partner(): return lax.ppermute(block, axis, route)]
    pallas_call x0 -> x1, Pallas kernels: none -> 75.4 us  [local(): pl.pallas_call(functools.partial(body, cfg), out_shape=tuple((jax.ShapeDt...]
    ppermute x7 -> x0, waiting for transfers between devices: 24.2 us -> none  [the longest x4 22.6 us: shifted(): return lax.ppermute(value, axis, pairs)]
  transfers between devices with their start and end apart: 8 -> 0, of which waited for: 5 -> 0; matrix products, arithmetic and copies ran while one was open for 0% -> 0% of each run, Pallas kernels for 0% -> 0%
where the time goes in v2:
time: 80.9 us; the launch traced here: 79.9 us
  Pallas kernels  75.4 us (93%)
  local copies, waits for them, and re-layouts  2.64 us (3%)
  between operations  1.93 us (2%)
    pallas_call x1, Pallas kernels, local(): pl.pallas_call(functools.partial(body, cfg), out_shape=tuple((jax.ShapeDt...  75.4 us
    unnamed x2, local copies, waits for them, and re-layouts  2.64 us

profile of v2, /device:TPU:1, one launch (start us, length us, event | category | flops | bytes accessed | tf_op | source)
XLA Modules:
  0.0 79.9 jit_solution(3669344830233648014)
XLA Ops:
  1.9 75.4 %shard_map.77 = (f32[6,576]{1,0:T(8,128)}, f32[4,576]{1,0:T(4,128)}) custom-call(f32[1]{0:T(128)S(6)} %copy.10.scale_ref, f32[1]{0:T(128)S(6)} %copy.11.bias_ref, bf16[256,1536]{1,0:T(8,128)(2,1)} %img_ref.1, bf16[256,1024]{1,0:T(8,128)(2,1)} %txt_ref.1, bf16[576,1536]{1,0:T(8,128)(2,1)} %bitcast.2, bf16[576,1024]{1,0:T(8,128)(2,1)} %bitcast.3), custom_call_target="tpu_custom_call" | custom-call | tf_op jit(solution)/shard_map/pallas_call | solution.py:395
  77.3 1.3 %copy.12 = f32[6,576]{1,0:T(8,128)} copy(f32[6,576]{1,0:T(8,128)} %get-tuple-element.4) | data formatting | bytes 27648
  78.6 1.3 %copy.13 = f32[4,576]{1,0:T(4,128)} copy(f32[4,576]{1,0:T(4,128)} %get-tuple-element.5) | data formatting | bytes 18432

commit v3 on v2

--- a/solution.py
+++ b/solution.py
@@ -405,17 +405,11 @@
 
 
 def column_chunks(cols):
-    return ((0, 256, False), (256, cols - 256, False))
+    return ((0, 192, False), (192, 256, True), (448, cols - 448, False))
 
 
 def stage_order(chunks):
-    steps = ["gc1l", "g1xl"]
-    out = []
-    for step in range(4 + len(chunks)):
-        for q, c in enumerate(chunks):
-            if 0 <= step - q < 4:
-                out.append((steps[c[2]][step - q], q))
-    return out
+    return (("g", 0), ("g", 1), ("g", 2), ("c", 0), ("1", 1), ("c", 2), ("1", 0), ("x", 1), ("1", 2), ("l", 0), ("l", 1), ("l", 2))
 
 
 def solution(mesh):

time: 80.9 us -> 75.4 us (0.932)
  Pallas kernels: 75.4 us -> 70.5 us
    pallas_call x1, Pallas kernels: 75.4 us -> 70.5 us  [local(): pl.pallas_call(functools.partial(body, cfg), out_shape=tuple((jax.ShapeDt...]
where the time goes in v3:
time: 75.4 us; the launch traced here: 75.1 us
  Pallas kernels  70.5 us (94%)
  local copies, waits for them, and re-layouts  2.64 us (4%)
  between operations  1.93 us (3%)
    pallas_call x1, Pallas kernels, local(): pl.pallas_call(functools.partial(body, cfg), out_shape=tuple((jax.ShapeDt...  70.5 us
    unnamed x2, local copies, waits for them, and re-layouts  2.64 us

profile of v3, /device:TPU:1, one launch (start us, length us, event | category | flops | bytes accessed | tf_op | source)
XLA Modules:
  0.0 75.1 jit_solution(11082453834954674715)
XLA Ops:
  1.9 70.5 %shard_map.77 = (f32[6,576]{1,0:T(8,128)}, f32[4,576]{1,0:T(4,128)}) custom-call(f32[1]{0:T(128)S(6)} %copy.10.scale_ref, f32[1]{0:T(128)S(6)} %copy.11.bias_ref, bf16[256,1536]{1,0:T(8,128)(2,1)} %img_ref.1, bf16[256,1024]{1,0:T(8,128)(2,1)} %txt_ref.1, bf16[576,1536]{1,0:T(8,128)(2,1)} %bitcast.2, bf16[576,1024]{1,0:T(8,128)(2,1)} %bitcast.3), custom_call_target="tpu_custom_call" | custom-call | tf_op jit(solution)/shard_map/pallas_call | solution.py:395
  72.4 1.3 %copy.12 = f32[6,576]{1,0:T(8,128)} copy(f32[6,576]{1,0:T(8,128)} %get-tuple-element.4) | data formatting | bytes 27648
  73.8 1.3 %copy.13 = f32[4,576]{1,0:T(4,128)} copy(f32[4,576]{1,0:T(4,128)} %get-tuple-element.5) | data formatting | bytes 18432

commit v4 on v3

--- a/solution.py
+++ b/solution.py
@@ -12,6 +12,7 @@
 EPS = 1e-06
 NX, NYH, CLS = 4, 2, 4
 MSGS = 128
+VMEM_BYTES = 53 * 2**20 + 6 * 2**17
 F32 = jnp.float32
 BF16 = jnp.bfloat16
 
@@ -30,9 +31,9 @@
 
 
 def body(cfg, scale_ref, bias_ref, img_ref, txt_ref, wi_ref, wt_ref, out_img, out_txt, *scratch):
-    (smem, feats, weights, perm, feats_t, fx, normed, own_t, own_n, win, acc) = scratch[:11]
-    (sq_out, sq_in, inner_out, inner_in, ssem, rsem, lsem) = scratch[11:18]
-    rest = scratch[18:]
+    (smem, feats, weights, perm, feats_t, fx, proj, own_t, own_n, win, acc) = scratch[:11]
+    (sq_out, sq_in, inner_out, inner_in, inv_mine, inv_win, ssem, rsem, lsem) = scratch[11:20]
+    rest = scratch[20:]
     dp, tok, widths, chunks = cfg["dp"], cfg["tok"], cfg["widths"], cfg["chunks"]
     zgs = dp // (NX * NYH * CLS)
     zs = zgs * CLS
@@ -73,6 +74,25 @@
     peers += [along_z(dz, dy) for dz in (1, -1, 2, -2) for dy in range(NYH)]
     peers += [dev for (j, dt), dev in last.items() if j]
     peers += list(x_dev.values()) + [along_z(0, 1), partner]
+
+    def loads(which):
+        f, w, n = (img_ref, txt_ref)[which], (wi_ref, wt_ref)[which], widths[which] // 2
+        out = []
+        for part in range(2):
+            k = pl.ds(part * n, n)
+            out.append(pltpu.make_async_copy(f.at[:, k], feats.at[:, k], lsem.at[2 * part]))
+            out.append(pltpu.make_async_copy(w.at[:, k], weights.at[:, k], lsem.at[2 * part + 1]))
+        out.append(pltpu.make_async_copy(scale_ref, smem.at[0], lsem.at[4]))
+        out.append(pltpu.make_async_copy(bias_ref, smem.at[1], lsem.at[5]))
+        return out
+
+    def start_loads(which):
+        for c in loads(which):
+            c.start()
+
+    for which in range(2):
+        pl.when(t == which)(functools.partial(start_loads, which))
+
     barrier = pltpu.get_barrier_semaphore()
     for dev in peers:
         pl.semaphore_signal(barrier, inc=1, device_id=dev, device_id_type=MESH)
@@ -98,18 +118,18 @@
             pl.when(t == which)(functools.partial(fn, which, *args))
 
     def project(which):
-        f, w, wide = (img_ref, txt_ref)[which], (wi_ref, wt_ref)[which], widths[which]
-        loads = [
-            pltpu.make_async_copy(f, feats.at[:, pl.ds(0, wide)], lsem.at[0]),
-            pltpu.make_async_copy(w, weights.at[:, pl.ds(0, wide)], lsem.at[1]),
-            pltpu.make_async_copy(scale_ref, smem.at[0], lsem.at[2]),
-            pltpu.make_async_copy(bias_ref, smem.at[1], lsem.at[3]),
-        ]
-        for c in loads:
-            c.start()
-        for c in loads:
-            c.wait()
-        normed[...] = dot_nt(weights[:, :wide], feats[:, :wide])
+        n = widths[which] // 2
+        ls = loads(which)
+        for part in range(2):
+            k = slice(part * n, part * n + n)
+            ls[2 * part].wait()
+            ls[2 * part + 1].wait()
+            if part == 0:
+                proj[...] = dot_nt(weights[:, k], feats[:, k])
+            else:
+                proj[...] += dot_nt(weights[:, k], feats[:, k])
+        ls[4].wait()
+        ls[5].wait()
 
     def reorder(which):
         wide, r = widths[which], pieces[which]
@@ -135,37 +155,58 @@
             send(("f", j), feats_t.at[xs], fx.at[x, pl.ds(0, rows)], x_dev[j], which, lambda: fx.at[0, pl.ds(0, rows)])
 
     by_tower(project)
-    squares = jnp.sum(normed[...] * normed[...], axis=0, keepdims=True)
+    value = proj[...]
+    squares = jnp.sum(value * value, axis=0, keepdims=True)
     sq_out[...] = jnp.broadcast_to(squares, sq_out.shape)
+    value = value.astype(BF16)
+    for th in range(2):
+        own_t[m, th] = value[:, th * half : (th + 1) * half]
     pl.semaphore_wait(barrier, len(peers))
+
+    cols = cfg["cols"]
+    cut = cols // 2
+    halves = (pl.ds(0, cut), pl.ds(cut, cols - cut))
     send("sq", sq_out, sq_in, partner)
-    arrive("sq", sq_in)
-    inv_radius = 1.0 / jnp.sqrt(squares + sq_in[:1] + EPS)
-    unit = normed[...] * inv_radius
-    normed[...] = unit
-    unit = unit.astype(BF16)
-    for th in range(2):
-        own_t[m, th] = unit[:, th * half : (th + 1) * half]
-
-    send("e0", own_t.at[m, 1 - h], own_t.at[m, 1 - h], partner)
+    for a in range(2):
+        send(("e0", a), own_t.at[m, 1 - h, halves[a]], own_t.at[m, 1 - h, halves[a]], partner)
     for s in (1, -1, 0):
         send(("b", s, 0), own_t.at[m, h], win.at[2 - s, m], cross[s])
     send("e1", own_t.at[m, h], own_t.at[m, h], partner)
+
+    arrive("sq", sq_in)
+    inv_radius = 1.0 / jnp.sqrt(squares + sq_in[:1] + EPS)
+    for th in range(2):
+        inv_mine[th] = jnp.broadcast_to(inv_radius[:, th * half : (th + 1) * half], (8, half))
+    for s in (1, -1, 0):
+        send(("r", s), inv_mine.at[h], inv_win.at[2 - s], cross[s])
+    inv_rows = jnp.transpose(jnp.broadcast_to(inv_radius, (half, tok)))
+
+    for a in range(2):
+        arrive(("e0", a), own_t.at[1 - m, h, halves[a]])
+        for s in (1, -1):
+            send(("b", s, 1 + a), own_t.at[1 - m, h, halves[a]], win.at[2 - s, 1 - m, halves[a]], cross[s])
+    send(("b", 0, 1), own_t.at[1 - m, h], win.at[2, 1 - m], cross[0])
+
+    def pass_on(s, f):
+        side = cross[-s][2]
+        c = side if f == 0 else 1 - side
+        part = pl.ds(0, cols) if f == 0 else halves[f - 1]
+        arrive(("b", s, f), win.at[2 - s, c, part])
+        send(("w", s, f), win.at[2 - s, c, part], win.at[2 - 2 * s, c, part], onward[s])
+
+    for s in (1, -1):
+        pass_on(s, 0)
+    for s in (1, -1):
+        arrive(("r", s), inv_win.at[2 - s])
+        send(("rw", s), inv_win.at[2 - s], inv_win.at[2 - 2 * s], onward[s])
+    arrive("e1", own_t.at[1 - m, 1 - h])
+    for f in (1, 2):
+        for s in (1, -1):
+            pass_on(s, f)
+    for c in range(2):
+        for th in range(2):
+            own_n[c, th * half : (th + 1) * half, :] = jnp.transpose(own_t[c, th])
     by_tower(reorder)
-    arrive("e0", own_t.at[1 - m, h])
-    for s in (1, -1, 0):
-        send(("b", s, 1), own_t.at[1 - m, h], win.at[2 - s, 1 - m], cross[s])
-    for f in range(2):
-        for s in (1, -1):
-            side = cross[-s][2]
-            c = side if f == 0 else 1 - side
-            arrive(("b", s, f), win.at[2 - s, c])
-            send(("w", s, f), win.at[2 - s, c], win.at[2 - 2 * s, c], onward[s])
-        if f == 0:
-            arrive("e1", own_t.at[1 - m, 1 - h])
-            for c in range(2):
-                for th in range(2):
-                    own_n[c, th * half : (th + 1) * half, :] = jnp.transpose(own_t[c, th])
 
     scale, bias = smem[0, 0], smem[1, 0]
     inv_scale = F32(1.0 / math.sqrt(tok * dp))
@@ -175,11 +216,15 @@
         if k == 0:
             for f in range(2):
                 arrive(("b", 0, f), win.at[slot, f])
+            arrive(("r", 0), inv_win.at[slot])
         if abs(k) == 2:
-            for f in range(2):
-                arrive(("w", -k // 2, f), win.at[slot, f])
-        dots = dot_nn(own_n[0], win[slot, 0]) + dot_nn(own_n[1], win[slot, 1])
-        logits = scale * dots + bias
+            arrive(("rw", -k // 2), inv_win.at[slot])
+            arrive(("w", -k // 2, 0), win.at[slot, 0])
+            for a in range(2):
+                arrive(("w", -k // 2, 1 + a), win.at[slot, 1, halves[a]])
+        dots = (dot_nn(own_n[0], win[slot, 0]) + dot_nn(own_n[1], win[slot, 1])) * inv_rows
+        inv_cols = inv_win[slot][:1]
+        logits = scale * (dots * inv_cols) + bias
         if k == 0:
             rows = lax.broadcasted_iota(jnp.int32, (tok, half), 0)
             columns = lax.broadcasted_iota(jnp.int32, (tok, half), 1) + h * half
@@ -187,7 +232,7 @@
             coef = -labels * jax.nn.sigmoid(-labels * logits) * inv_scale
         else:
             coef = jax.nn.sigmoid(logits) * inv_scale
-        coef = coef.astype(BF16)
+        coef = (coef * inv_cols).astype(BF16)
         inner = inner + coef.astype(F32) * dots
         for c in range(2):
             term = dot_nt(win[slot, c], coef)
@@ -209,7 +254,7 @@
         b = buf[q]
         arrive(("p", q), b["pr"])
         grad = scale * acc[m, c0 : c0 + w] + b["pr"][...].astype(F32)
-        grad = (grad - normed[c0 : c0 + w] * total_inner) * inv_radius
+        grad = (grad - proj[c0 : c0 + w] * (inv_radius * total_inner)) * inv_radius
         own = 0 if z_first else x
         b["gx"][own] = grad.astype(BF16)
         if z_first:
@@ -348,7 +393,7 @@
     widths = (img_feats.shape[1], txt_feats.shape[1])
     cols = w_img.shape[1]
     chunks = cfg["chunks"](cols)
-    cfg = dict(cfg, dp=dp, tok=tok, widths=widths, chunks=chunks)
+    cfg = dict(cfg, cols=cols, dp=dp, tok=tok, widths=widths, chunks=chunks)
     zgs = dp // (NX * NYH * CLS)
     half = tok // 2
     wide = max(widths)
@@ -371,9 +416,11 @@
         pltpu.VMEM((8, tok), F32),
         pltpu.VMEM((8, tok), F32),
         pltpu.VMEM((8, tok), F32),
+        pltpu.VMEM((2, 8, half), F32),
+        pltpu.VMEM((5, 8, half), F32),
         pltpu.SemaphoreType.DMA((MSGS,)),
         pltpu.SemaphoreType.DMA((MSGS,)),
-        pltpu.SemaphoreType.DMA((4,)),
+        pltpu.SemaphoreType.DMA((6,)),
     ]
     for _, w, z_first in chunks:
         xb = NX if z_first else 1
@@ -399,13 +446,13 @@
         out_specs=(vmem, vmem),
         scratch_shapes=scratch,
         compiler_params=pltpu.CompilerParams(
-            collective_id=0, has_side_effects=True, vmem_limit_bytes=61 * 1024 * 1024
+            collective_id=0, has_side_effects=True, vmem_limit_bytes=VMEM_BYTES
         ),
     )(logit_scale, logit_bias, img_feats, txt_feats, w_img.T, w_txt.T)
 
 
 def column_chunks(cols):
-    return ((0, 192, False), (192, 256, True), (448, cols - 448, False))
+    return ((0, 256, False), (256, 128, True), (384, cols - 384, False))
 
 
 def stage_order(chunks):

time: 75.4 us -> 71.2 us (0.944)
  Pallas kernels: 70.5 us -> 67.9 us
  local copies, waits for them, and re-layouts: 2.64 us -> 1.21 us
    pallas_call x1, Pallas kernels: 70.5 us -> 67.9 us  [local(): pl.pallas_call(functools.partial(body, cfg), out_shape=tuple((jax.ShapeDt...]
    unnamed x2, local copies, waits for them, and re-layouts: 2.64 us -> 1.21 us
where the time goes in v4:
time: 71.2 us; the launch traced here: 71.1 us
  Pallas kernels  67.9 us (95%)
  between operations  1.93 us (3%)
  local copies, waits for them, and re-layouts  1.21 us (2%)
    pallas_call x1, Pallas kernels, local(): pl.pallas_call(functools.partial(body, cfg), out_shape=tuple((jax.ShapeDt...  67.9 us

profile of v4, /device:TPU:1, one launch (start us, length us, event | category | flops | bytes accessed | tf_op | source)
XLA Modules:
  0.0 71.1 jit_solution(323534255042567744)
XLA Ops:
  1.9 67.9 %shard_map.77 = (f32[6,576]{1,0:T(8,128)S(1)}, f32[4,576]{1,0:T(4,128)S(1)}) custom-call(f32[1]{0:T(128)S(6)} %copy.10.scale_ref, f32[1]{0:T(128)S(6)} %copy.11.bias_ref, bf16[256,1536]{1,0:T(8,128)(2,1)} %img_ref.1, bf16[256,1024]{1,0:T(8,128)(2,1)} %txt_ref.1, bf16[576,1536]{1,0:T(8,128)(2,1)} %bitcast.2, bf16[576,1024]{1,0:T(8,128)(2,1)} %bitcast.3), custom_call_target="tpu_custom_call" | custom-call | tf_op jit(solution)/shard_map/pallas_call | solution.py:442
  69.9 0.6 copy.12
  70.5 0.6 copy.13

commit v5 on v4

--- a/solution.py
+++ b/solution.py
@@ -12,6 +12,7 @@
 EPS = 1e-06
 NX, NYH, CLS = 4, 2, 4
 MSGS = 128
+ORDER = ("g0", "g1", "g2", "g3", "c0", "11", "c2", "10", "c3", "x1", "12", "13", "l0", "l1", "l2", "l3")
 VMEM_BYTES = 53 * 2**20 + 6 * 2**17
 F32 = jnp.float32
 BF16 = jnp.bfloat16
@@ -206,8 +207,6 @@
     for c in range(2):
         for th in range(2):
             own_n[c, th * half : (th + 1) * half, :] = jnp.transpose(own_t[c, th])
-    by_tower(reorder)
-
     scale, bias = smem[0, 0], smem[1, 0]
     inv_scale = F32(1.0 / math.sqrt(tok * dp))
     inner = jnp.zeros((tok, half), F32)
@@ -217,6 +216,8 @@
             for f in range(2):
                 arrive(("b", 0, f), win.at[slot, f])
             arrive(("r", 0), inv_win.at[slot])
+        if n == 3:
+            by_tower(reorder)
         if abs(k) == 2:
             arrive(("rw", -k // 2), inv_win.at[slot])
             arrive(("w", -k // 2, 0), win.at[slot, 0])
@@ -452,11 +453,11 @@
 
 
 def column_chunks(cols):
-    return ((0, 256, False), (256, 128, True), (384, cols - 384, False))
+    return ((0, 128, False), (128, 128, True), (256, 128, False), (384, cols - 384, False))
 
 
 def stage_order(chunks):
-    return (("g", 0), ("g", 1), ("g", 2), ("c", 0), ("1", 1), ("c", 2), ("1", 0), ("x", 1), ("1", 2), ("l", 0), ("l", 1), ("l", 2))
+    return tuple((s[0], int(s[1])) for s in ORDER)
 
 
 def solution(mesh):

time: 71.2 us -> 70.4 us (0.989)
  Pallas kernels: 67.9 us -> 67.1 us
    pallas_call x1, Pallas kernels: 67.9 us -> 67.1 us  [local(): pl.pallas_call(functools.partial(body, cfg), out_shape=tuple((jax.ShapeDt...]
where the time goes in v5:
time: 70.4 us; the launch traced here: 70.3 us
  Pallas kernels  67.1 us (95%)
  between operations  1.93 us (3%)
  local copies, waits for them, and re-layouts  1.21 us (2%)
    pallas_call x1, Pallas kernels, local(): pl.pallas_call(functools.partial(body, cfg), out_shape=tuple((jax.ShapeDt...  67.1 us

profile of v5, /device:TPU:1, one launch (start us, length us, event | category | flops | bytes accessed | tf_op | source)
XLA Modules:
  0.0 70.3 jit_solution(3891920164582704651)
XLA Ops:
  1.9 67.1 %shard_map.77 = (f32[6,576]{1,0:T(8,128)S(1)}, f32[4,576]{1,0:T(4,128)S(1)}) custom-call(f32[1]{0:T(128)S(6)} %copy.10.scale_ref, f32[1]{0:T(128)S(6)} %copy.11.bias_ref, bf16[256,1536]{1,0:T(8,128)(2,1)} %img_ref.1, bf16[256,1024]{1,0:T(8,128)(2,1)} %txt_ref.1, bf16[576,1536]{1,0:T(8,128)(2,1)} %bitcast.2, bf16[576,1024]{1,0:T(8,128)(2,1)} %bitcast.3), custom_call_target="tpu_custom_call" | custom-call | tf_op jit(solution)/shard_map/pallas_call | solution.py:443
  69.1 0.6 copy.12
  69.7 0.6 copy.13
